TPU v7x, 32 devices: a whole 2x2x4 slice. The times are simulated.
32 devices in a mesh: ens: 4 (over y, core), trc: 8 (over z, x).
Axes of the slice: x: 2, y: 2, z: 4, core: 2. Of those that a mesh axis runs over, the one named last changes fastest.
Arguments:
- tracer_state: bfloat16 [1536, 4, 8, 1440], P(('ens', 'trc')), may hold values from -6 to 6
- velocity: float32 [2, 4, 8, 1440], replicated, may hold values from -0.24 to 0.24
- land_mask: int32 [8, 1440], replicated, may hold values from 0 to 1, as said below
- in_weight: bfloat16 [24, 256], replicated, may hold values from -1.25 to 1.25
- bias_one: float32 [256], replicated, may hold values from -3 to 3
- hid_weight: bfloat16 [256, 256], replicated, may hold values from -0.375 to 0.375
- bias_two: float32 [256], replicated, may hold values from -3 to 3
- out_coef: float32 [64, 24, 256], P('ens'), may hold values from -6 to 6
- obs_cell: int32 [8, 128], P('trc'), may hold values from 0 to 5759, as said below
- obs_count: int32 [8], P('trc'), may hold values from 16 to 128, as said below
- obs_value: float32 [8, 6, 128], P('trc'), may hold values from -6 to 6
- obs_var: float32 [8, 6, 128], P('trc'), may hold values from 0.05 to 0.5
- obs_noise: float32 [64, 8, 6, 128], P(None, 'trc'), may hold values from -2 to 2
Outputs:
- new_state: bfloat16 [1536, 4, 8, 1440], P('ens', None, 'trc')
- new_coef: float32 [64, 24, 256], P('ens')
Inputs may be any that keep to these rules, and one draw needn't show every extreme that they name: `land_mask`: every block of 1 latitude rows (rows k * 1 to (k + 1) - 1) holds at most 1152 ocean columns, and some block exactly 1152. `obs_cell`: every slot names an ocean cell of its block. `obs_count`: some block uses all 128 slots.
All inputs are finite; a program needn't handle non-finite values.
Results may differ from a plain program's by a relative error of at most 0.0068.
Values may be sent and summed in bfloat16 or wider, within the bound.
A program may use at most 128 MiB of HBM per device.

v0:
```python
import jax
import jax.numpy as jnp
from jax import lax
from jax.sharding import PartitionSpec as P

OBS_TR = 6
ADV_STEPS = 2
OBS_CAP = 128


def transport(concentration, velocity, sea_mask):
    east_open = sea_mask * jnp.roll(sea_mask, -1, axis=1)
    north_open = sea_mask * jnp.concatenate([sea_mask[1:], jnp.zeros_like(sea_mask[:1])], axis=0)
    east_speed = velocity[0] * east_open
    north_speed = velocity[1] * north_open
    for _ in range(ADV_STEPS):
        east_value = jnp.roll(concentration, -1, axis=-1)
        east_flux = (
            jnp.maximum(east_speed, 0.0) * concentration + jnp.minimum(east_speed, 0.0) * east_value
        )
        north_value = jnp.concatenate(
            [concentration[..., 1:, :], jnp.zeros_like(concentration[..., :1, :])], axis=-2
        )
        north_flux = (
            jnp.maximum(north_speed, 0.0) * concentration
            + jnp.minimum(north_speed, 0.0) * north_value
        )
        west_flux = jnp.roll(east_flux, 1, axis=-1)
        south_flux = jnp.concatenate(
            [jnp.zeros_like(north_flux[..., :1, :]), north_flux[..., :-1, :]], axis=-2
        )
        concentration = concentration - (east_flux - west_flux) - (north_flux - south_flux)
    return concentration


def reaction(fields, in_weight, bias_one, hid_weight, bias_two, member_coef, sea_cells):
    contract = (((0,), (0,)), ((), ()))
    hidden_one = lax.dot_general(in_weight, fields, contract, preferred_element_type=jnp.float32)
    hidden_one = jax.nn.silu(hidden_one + bias_one[:, None]).astype(jnp.bfloat16)
    hidden_two = lax.dot_general(
        hid_weight, hidden_one, contract, preferred_element_type=jnp.float32
    )
    hidden_two = jax.nn.silu(hidden_two + bias_two[:, None]).astype(jnp.bfloat16)
    tendency = jnp.dot(
        member_coef, hidden_two, preferred_element_type=jnp.float32
    ) * hid_weight.shape[0] ** (-0.5)
    return ((fields.astype(jnp.float32) + tendency) * sea_cells).astype(jnp.bfloat16)


def solve_system(system, right_side):
    factor = jnp.linalg.cholesky(system)
    middle = lax.linalg.triangular_solve(factor, right_side, left_side=True, lower=True)
    return lax.linalg.triangular_solve(factor, middle, left_side=True, lower=True, transpose_a=True)


def shards(
    tracer_state,
    velocity,
    land_mask,
    in_weight,
    bias_one,
    hid_weight,
    bias_two,
    out_coef,
    obs_cell,
    obs_count,
    obs_value,
    obs_var,
    obs_noise,
):
    blocks = lax.axis_size("trc")
    own_block = lax.axis_index("trc")
    group_index = lax.axis_index("ens")
    field_rows, levels, lat_rows, lon_count = tracer_state.shape
    row_block = lat_rows // blocks
    block_width = row_block * lon_count
    members_here = out_coef.shape[0]
    tracers = in_weight.shape[0]
    group_rows = members_here * tracers
    highest = lax.Precision.HIGHEST
    sea_mask = land_mask.astype(jnp.float32)
    advected = transport(tracer_state.astype(jnp.float32) * sea_mask, velocity, sea_mask).astype(
        jnp.bfloat16
    )
    coef_half = out_coef.astype(jnp.bfloat16)
    sea_own = lax.dynamic_slice_in_dim(sea_mask, own_block * row_block, row_block, 0)
    gathered = lax.all_to_all(advected, "trc", split_axis=2, concat_axis=0, tiled=True)
    out_shape = gathered.shape
    grouped = gathered.reshape(members_here, tracers, -1)
    sea_cells = jnp.broadcast_to(sea_own[None], (out_shape[1],) + sea_own.shape).reshape(-1)

    def one_member(inputs):
        fields, member_coef = inputs
        return reaction(fields, in_weight, bias_one, hid_weight, bias_two, member_coef, sea_cells)

    reacted = lax.map(one_member, (grouped, coef_half))
    new_cols = reacted.reshape(out_shape)
    new_flat = new_cols.reshape(group_rows, levels, block_width)
    observed = new_flat.reshape(members_here, tracers, levels * block_width)[:, :OBS_TR]
    cell_index = jnp.broadcast_to(obs_cell[0][None, None], (members_here, OBS_TR, OBS_CAP))
    predicted_own = jnp.take_along_axis(observed, cell_index, axis=2)
    predicted_all = lax.all_gather(predicted_own, "ens", axis=0, tiled=True)
    member_total = predicted_all.shape[0]
    slot_ids = jnp.arange(OBS_CAP, dtype=jnp.int32)
    valid_slots = (slot_ids < obs_count[0]).astype(jnp.float32)
    weight = valid_slots[None, :] / obs_var[0]
    guessed = predicted_all.astype(jnp.float32).reshape(member_total, -1)
    anomaly = guessed - jnp.mean(guessed, axis=0)
    misfit = (obs_value[None] + obs_noise).reshape(member_total, -1) - guessed
    weighted = anomaly * weight.reshape(1, -1)
    gram_part = jnp.dot(weighted, anomaly.T, precision=highest, preferred_element_type=jnp.float32)
    cross_part = jnp.dot(weighted, misfit.T, precision=highest, preferred_element_type=jnp.float32)
    gram, cross = lax.psum((gram_part, cross_part), "trc")
    system = (member_total - 1) * jnp.eye(member_total, dtype=jnp.float32) + gram
    mixing = solve_system(system, cross)
    flat_coef = out_coef.reshape(members_here, -1)
    first_member = group_index * members_here
    mixing_rows = lax.dynamic_slice_in_dim(mixing, first_member, members_here, 0)
    summed = lax.psum_scatter(
        jnp.dot(mixing_rows.T, flat_coef, precision=highest, preferred_element_type=jnp.float32),
        "ens",
        scatter_dimension=0,
        tiled=True,
    )
    new_coef = flat_coef + summed
    return (new_cols, new_coef.reshape(members_here, tracers, -1))


def solution(mesh):
    in_specs = (
        P(("ens", "trc"), None, None, None),
        P(),
        P(),
        P(),
        P(),
        P(),
        P(),
        P("ens", None, None),
        P("trc", None),
        P("trc"),
        P("trc", None, None),
        P("trc", None, None),
        P(None, "trc", None, None),
    )
    out_specs = (P("ens", None, "trc", None), P("ens", None, None))
    return jax.shard_map(shards, mesh=mesh, in_specs=in_specs, out_specs=out_specs, check_vma=False)
```

profile of v0, /device:TPU:0, one launch (start us, length us, event | category | flops | bytes accessed | tf_op | source)
XLA Modules:
  0.0 595.0 jit_solution(9890008790325714508)
XLA Ops:
  8.1 5.2 convert_multiply_fusion
  14.4 6.1 %slice.97 = f32[48,4,8,1439]{3,0,1,2:T(8,128)} slice(f32[48,4,8,1440]{3,0,1,2:T(8,128)S(1)} %convert_multiply_fusion), slice={[0:48], [0:4], [0:8], [1:1440]} | slice | bytes 17682432 | tf_op jit(solution)/shard_map/jit(_roll_static)/slice | solution.py:17
  21.4 13.6 %multiply_add_fusion.1 = (f32[48,4,8,1440]{3,0,1,2:T(8,128)}, f32[48,4,8,1440]{3,0,1,2:T(8,128)S(1)}) fusion(f32[48,4,7,1440]{3,0,1,2:T(8,128)S(1)} %slice.102, f32[4,8,1440]{2,0,1:T(4,128)S(1)} %copy.61, f32[4,8,1440]{2,0,1:T(4,128)S(1)} %copy.60, f32[8,1440]{1,0:T(8,128)S(1)} %convert_element_type.36, bf16[48,4,8,1440]{3,2,1,0:T(8,128)(2,1)} %param.15, ...), kind=kLoop, calls=%fused_computation.34 | loop fusion | flops 19906560 | bytes 39490560 | tf_op jit(solution)/shard_map/add | solution.py:25
  35.0 11.1 %slice.103 = f32[48,4,7,1440]{3,0,1,2:T(8,128)} slice(f32[48,4,8,1440]{3,0,1,2:T(8,128)} %get-tuple-element.103), slice={[0:48], [0:4], [0:7], [0:1440]} | slice | bytes 15482880 | tf_op jit(solution)/shard_map/slice | solution.py:30
  46.4 15.1 %fusion.18 = f32[48,4,8,1440]{3,0,1,2:T(8,128)S(1)} fusion(f32[48,4,8,1440]{3,0,1,2:T(8,128)} %copy-done, f32[48,4,8,1439]{3,0,1,2:T(8,128)} %bitcast.106, f32[48,4,8,1]{3,0,1,2:T(8,128)S(1)} %slice.99, f32[48,4,7,1440]{3,0,1,2:T(8,128)} %slice.103, f32[8,1440]{1,0:T(8,128)S(1)} %convert_element_type.36, bf16[48,4,8,1440]{3,2,1,0:T(8,128)(2,1)} %param.15, ...), kind=kLoop, calls=%fused_computation.26 | loop fusion | flops 22118400 | bytes 46863360 | tf_op jit(solution)/shard_map/sub | solution.py:32
  61.5 6.1 %slice.104 = f32[48,4,8,1439]{3,0,1,2:T(8,128)} slice(f32[48,4,8,1440]{3,0,1,2:T(8,128)S(1)} %fusion.18), slice={[0:48], [0:4], [0:8], [1:1440]} | slice | bytes 17682432 | tf_op jit(solution)/shard_map/jit(_roll_static)/slice | solution.py:17
  71.9 17.3 %multiply_add_fusion = (f32[48,4,8,1440]{3,0,1,2:T(8,128)}, f32[48,4,8,1440]{3,0,1,2:T(8,128)}) fusion(f32[48,4,7,1440]{3,0,1,2:T(8,128)} %slice.108, f32[48,4,8,1440]{3,0,1,2:T(8,128)S(1)} %fusion.18, f32[4,8,1440]{2,0,1:T(4,128)S(1)} %copy.61, f32[4,8,1440]{2,0,1:T(4,128)S(1)} %copy.60, f32[48,4,8,1]{3,0,1,2:T(8,128)S(1)} %slice.105, ...), kind=kLoop, calls=%fused_computation.33 | loop fusion | flops 15482880 | bytes 43868160 | tf_op jit(solution)/shard_map/add | solution.py:25
  89.3 7.8 %slice.109 = f32[48,4,7,1440]{3,0,1,2:T(8,128)} slice(f32[48,4,8,1440]{3,0,1,2:T(8,128)} %get-tuple-element.101), slice={[0:48], [0:4], [0:7], [0:1440]} | slice | bytes 15482880 | tf_op jit(solution)/shard_map/slice | solution.py:30
  98.5 15.8 %fusion.22 = bf16[48,4,8,1440]{3,0,1,2:T(8,128)(2,1)} fusion(f32[48,4,8,1440]{3,0,1,2:T(8,128)S(1)} %fusion.18, f32[48,4,8,1440]{3,0,1,2:T(8,128)} %get-tuple-element.102, f32[48,4,8,1439]{3,0,1,2:T(8,128)} %bitcast.107, f32[48,4,8,1]{3,0,1,2:T(8,128)S(1)} %slice.106, f32[48,4,7,1440]{3,0,1,2:T(8,128)} %slice.109, f32[48,4,7,1440]{3,0,1,2:T(8,128)} %slice.108, ...), kind=kLoop, calls=%fused_computation.32 | loop fusion | flops 19906560 | bytes 46817280 | tf_op jit(solution)/shard_map/convert_element_type | solution.py:82
  114.3 7.4 %all-to-all-start = ((bf16[48,4,8,1440]{3,0,1,2:T(8,128)(2,1)}), bf16[48,4,8,1440]{3,0,1,2:T(8,128)(2,1)}, u32[]{:S(2)}, u32[]{:S(2)}) async-start(bf16[48,4,8,1440]{3,0,1,2:T(8,128)(2,1)} %fusion.22), calls=%async_computation | async-start | bytes 9437184 | tf_op jit(solution)/shard_map/all_to_all | solution.py:87
  122.8 103.4 %all-to-all-done = bf16[48,4,8,1440]{3,0,1,2:T(8,128)(2,1)} async-done(((bf16[48,4,8,1440]{3,0,1,2:T(8,128)(2,1)}), bf16[48,4,8,1440]{3,0,1,2:T(8,128)(2,1)}, u32[]{:S(2)}, u32[]{:S(2)}) %all-to-all-start) | async-done | bytes 4423712 | tf_op jit(solution)/shard_map/all_to_all | solution.py:87
  226.2 8.1 %copy.62 = bf16[8,48,4,1,1440]{4,2,1,0,3:T(4,128)(2,1)} copy(bf16[8,48,4,1,1440]{4,1,2,0,3:T(8,128)(2,1)} %bitcast.5) | data formatting | bytes 8847360 | tf_op jit(solution)/shard_map/all_to_all | solution.py:87
  234.4 8.9 %reshape.106 = bf16[16,24,5760]{2,1,0:T(8,128)(2,1)} reshape(bf16[8,48,4,1,1440]{4,2,1,0,3:T(4,128)(2,1)} %copy.62) | data formatting | bytes 8847360 | tf_op jit(solution)/shard_map/reshape | solution.py:89
  243.2 141.9 %while.11 = (s32[]{:T(128)}, bf16[16,24,5760]{2,1,0:T(8,128)(2,1)}, bf16[16,24,5760]{2,1,0:T(8,128)(2,1)}, bf16[16,24,256]{2,1,0:T(8,128)(2,1)S(1)}, bf16[24,256...) while((s32[]{:T(128)}, bf16[16,24,5760]{2,1,0:T(8,128)(2,1)}, ...), condition=%wide.region_1.2_spmd.clone, body=%wide.region_0.1_spmd.clone.sunk | while | flops 914918400 | bytes 6986469 | solution.py:96
  292.1 4.4 fusion.60
  336.4 4.4 fusion.60
  386.6 116.4 %gather_fusion = bf16[12288]{0:T(1024)(128)(2,1)S(1)} fusion(bf16[16,6,5760]{2,1,0:T(8,128)(2,1)S(1)} %slice.91, s32[12288]{0:T(1024)S(1)} %reshape.111), kind=kCustom, calls=%fused_computation | custom fusion | bytes 196608 | tf_op jit(solution)/shard_map/jit(take_along_axis)/gather | solution.py:101
  503.1 5.3 all_gather.3
  509.3 35.7 %all-reduce.5 = (f32[64,64]{1,0:T(8,128)S(1)}, f32[64,64]{1,0:T(8,128)S(1)}) all-reduce(f32[64,64]{1,0:T(8,128)S(1)} %fusion.25, f32[64,64]{1,0:T(8,128)S(1)} %convolution_bitcast_fusion), channel_id=1, replica_groups=mesh['ens'=4,'trc'=8] {'trc'}, use_global_device_ids=true, to_apply=%region_6.7 | all-reduce | flops 8192 | bytes 65536 | tf_op jit(solution)/shard_map/psum | solution.py:113
  545.1 5.9 cholesky.16
  552.3 4.9 custom-call.8
  560.3 10.5 %reshape.107 = bf16[384,4,1,1440]{3,1,0,2:T(4,128)(2,1)} reshape(bf16[16,24,5760]{2,1,0:T(8,128)(2,1)} %get-tuple-element.49) | data formatting | bytes 8847360 | tf_op jit(solution)/shard_map/reshape | solution.py:97
  570.8 8.9 %copy.68 = bf16[384,4,1,1440]{0,3,2,1:T(8,128)(2,1)} copy(bf16[384,4,1,1440]{3,1,0,2:T(4,128)(2,1)} %reshape.107) | data formatting | bytes 8847360
  579.6 6.2 %reduce-scatter.2.cloned.1.call-done = f32[16,6144]{1,0:T(8,128)} async-done(((f32[64,6144]{1,0:T(8,128)}), f32[16,6144]{1,0:T(8,128)}) %reduce-scatter.2.cloned.1.call-update) | async-done | bytes 393232 | tf_op jit(solution)/shard_map/reduce_scatter | solution.py:119
  (138 shorter events, 150.8 us)
Async XLA Ops:
  14.4 7.0 %copy-start.1 = (f32[48,4,7,1440]{3,0,1,2:T(8,128)}, f32[48,4,7,1440]{3,0,1,2:T(8,128)S(1)}, u32[]{:S(2)}) copy-start(f32[48,4,7,1440]{3,0,1,2:T(8,128)S(1)} %slice.102) | copy-start | bytes 23224324
  14.4 6.3 %copy-start.5 = (s32[8,1440]{1,0:T(8,128)S(1)}, s32[8,1440]{1,0:T(8,128)}, u32[]{:S(2)}) copy-start(s32[8,1440]{1,0:T(8,128)} %param.17) | copy-start | bytes 138244
  14.4 6.3 %copy-start.3 = (f32[2,4,8,1440]{3,2,1,0:T(8,128)S(1)}, f32[2,4,8,1440]{3,2,1,0:T(8,128)}, u32[]{:S(2)}) copy-start(f32[2,4,8,1440]{3,2,1,0:T(8,128)} %param.16) | copy-start | bytes 1105924
  35.0 11.4 %copy-start = (f32[48,4,8,1440]{3,0,1,2:T(8,128)}, f32[48,4,8,1440]{3,0,1,2:T(8,128)S(1)}, u32[]{:S(2)}) copy-start(f32[48,4,8,1440]{3,0,1,2:T(8,128)S(1)} %get-tuple-element.104) | copy-start | bytes 26542084
  114.3 7.5 %copy-start.2 = (f32[16,24,256]{2,1,0:T(8,128)S(1)}, f32[16,24,256]{2,1,0:T(8,128)}, u32[]{:S(2)}) copy-start(f32[16,24,256]{2,1,0:T(8,128)} %param.22) | copy-start | bytes 1179652
  114.3 7.5 %copy-start.8 = (s32[1,128]{1,0:T(1,128)S(1)}, s32[1,128]{1,0:T(1,128)}, u32[]{:S(2)}) copy-start(s32[1,128]{1,0:T(1,128)} %param.23) | copy-start | bytes 1540
  114.3 8.2 %copy-start.6 = (f32[1,6,128]{2,0,1:T(1,128)S(1)}, f32[1,6,128]{2,0,1:T(1,128)}, u32[]{:S(2)}) copy-start(f32[1,6,128]{2,0,1:T(1,128)} %param.25) | copy-start | bytes 9220
  114.3 8.5 %copy-start.7 = (f32[1,6,128]{2,0,1:T(1,128)S(1)}, f32[1,6,128]{2,0,1:T(1,128)}, u32[]{:S(2)}) copy-start(f32[1,6,128]{2,0,1:T(1,128)} %param.26) | copy-start | bytes 9220
  114.3 111.9 %all-to-all-start = ((bf16[48,4,8,1440]{3,0,1,2:T(8,128)(2,1)}), bf16[48,4,8,1440]{3,0,1,2:T(8,128)(2,1)}, u32[]{:S(2)}, u32[]{:S(2)}) async-start(bf16[48,4,8,1440]{3,0,1,2:T(8,128)(2,1)} %fusion.22), calls=%async_computation | async-start | bytes 9437184 | tf_op jit(solution)/shard_map/all_to_all | solution.py:87
  121.7 464.2 %reduce-scatter.2.cloned.1.call-start = ((), (), s32[]{:S(2)}) async-start(), calls=%async_computation.2 | async-start | bytes 1966080 | tf_op jit(solution)/shard_map/reduce_scatter | solution.py:119
  122.7 120.6 %copy-start.9 = (bf16[256,256]{1,0:T(8,128)(2,1)S(1)}, bf16[256,256]{1,0:T(8,128)(2,1)}, u32[]{:S(2)}) copy-start(bf16[256,256]{1,0:T(8,128)(2,1)} %param.20) | copy-start | bytes 393220
  122.7 120.6 %copy-start.10 = (bf16[24,256]{1,0:T(8,128)(2,1)S(1)}, bf16[24,256]{1,0:T(8,128)(2,1)}, u32[]{:S(2)}) copy-start(bf16[24,256]{1,0:T(8,128)(2,1)} %param.18) | copy-start | bytes 36868
  122.7 120.5 %copy-start.11 = (f32[256]{0:T(256)S(1)}, f32[256]{0:T(256)}, u32[]{:S(2)}) copy-start(f32[256]{0:T(256)} %param.19) | copy-start | bytes 3076
  122.7 120.5 %copy-start.12 = (f32[256]{0:T(256)S(1)}, f32[256]{0:T(256)}, u32[]{:S(2)}) copy-start(f32[256]{0:T(256)} %param.21) | copy-start | bytes 3076
  386.6 121.9 %copy-start.4 = (f32[64,1,6,128]{3,1,2,0:T(1,128)S(1)}, f32[64,1,6,128]{3,1,2,0:T(1,128)}, u32[]{:S(2)}) copy-start(f32[64,1,6,128]{3,1,2,0:T(1,128)} %param.27) | copy-start | bytes 589828
Sparse Core Ops, SparseCore 0:
  560.4 25.4 reduce-scatter.1
where the time goes:
time: 602 us; the launch traced here: 595 us
  local copies, waits for them, and re-layouts  197 us (33%)
  matrix products  143 us (24%)
  waiting for transfers between devices  110 us (18%)
  other arithmetic  81.2 us (13%)
  blocking collectives  41 us (7%)
  between operations  15.6 us (3%)
  starting transfers between devices  7.43 us (1%)
    gather x3, local copies, waits for them, and re-layouts, shards(): predicted_own = jnp.take_along_axis(observed, cell_index, axis=2)  116 us
    all_to_all x1, waiting for transfers between devices, shards(): lax.all_to_all(advected, 'trc', split_axis=2, concat_axis=0, tiled=True)  103 us
    dot_general x16, matrix products, reaction(): jnp.dot(member_coef, hidden_two, preferred_element_type=jnp.float32)  70.3 us
    dot_general x16, matrix products, reaction(): lax.dot_general(in_weight, fields, contract, preferred_element_type=jnp.f...  69.5 us
    psum x1, blocking collectives, shards(): gram, cross = lax.psum((gram_part, cross_part), 'trc')  35.7 us
    add x2, other arithmetic, transport(): jnp.maximum(north_speed, 0.0) * concentration  30.9 us
    slice x2, local copies, waits for them, and re-layouts, transport(): north_flux[..., :-1, :]  18.9 us
    convert_element_type x1, other arithmetic, shards(): transport(tracer_state.astype(jnp.float32) * sea_mask, velocity, sea_mask)  15.8 us
  transfers between devices with their start and end apart: 2, of which 2 were waited for; matrix products, arithmetic and copies ran while one was open for 3% of the time, Pallas kernels for 0%

commit v1 on v0

v1 whole, which is shorter than its diff:
```python
import functools

import jax
import jax.numpy as jnp
from jax import lax
from jax.experimental import pallas as pl
from jax.experimental.pallas import tpu as pltpu
from jax.sharding import PartitionSpec as P

OBS_TR = 6
ADV_STEPS = 2
OBS_CAP = 128
ROW_OCEAN = 1152
CHUNKS = 2
LANES = 128
FIELD_STEP = 4
WIDE = 384


def wrap_pad(buf, width):
    wide = buf.shape[-1]
    last = wide - LANES
    own = width - last
    tail = buf[..., last:]
    axis = tail.ndim - 1
    lane = lax.broadcasted_iota(jnp.int32, tail.shape, axis)
    east = pltpu.roll(buf[..., :LANES], own, axis)
    west = pltpu.roll(tail, LANES - own, axis)
    tail = jnp.where(lane < own, tail, jnp.where(lane < LANES - own, east, west))
    return jnp.concatenate([buf[..., :last], tail], axis=axis)


def transport_kernel(state_ref, velocity_ref, mask_ref, rank_ref, out_ref, coef, row, small, moved):
    fields, levels, lats, width = state_ref.shape
    wide = small.shape[-1]
    step_id = pl.program_id(0)

    @pl.when(step_id == 0)
    def _():
        small[:, :width] = mask_ref[...].astype(jnp.float32)
        sea = wrap_pad(small[...], width)
        row_ids = lax.broadcasted_iota(jnp.int32, sea.shape, 0)
        east_open = sea * pltpu.roll(sea, wide - 1, 1)
        north_open = jnp.where(row_ids < lats - 1, sea * pltpu.roll(sea, lats - 1, 0), 0.0)
        for level in range(levels):
            small[:, :width] = velocity_ref[0, level]
            east = wrap_pad(small[...], width) * east_open
            small[:, :width] = velocity_ref[1, level]
            north = wrap_pad(small[...], width) * north_open
            from_west = pltpu.roll(jnp.maximum(east, 0.0), 1, 1)
            from_south = pltpu.roll(jnp.maximum(north, 0.0), 1, 0)
            back_west = pltpu.roll(jnp.minimum(east, 0.0), 1, 1)
            back_south = pltpu.roll(jnp.minimum(north, 0.0), 1, 0)
            keep = 1.0 - (jnp.maximum(east, 0.0) - back_west)
            keep = keep - (jnp.maximum(north, 0.0) - back_south)
            coef[level, 0] = keep
            coef[level, 1] = -jnp.minimum(east, 0.0)
            coef[level, 2] = from_west
            coef[level, 3] = -jnp.minimum(north, 0.0)
            coef[level, 4] = from_south
            coef[level, 5] = sea

        for level in range(levels):

            def body(index, carry):
                first = index * FIELD_STEP
                row[..., :width] = state_ref[pl.ds(first, FIELD_STEP), level].astype(jnp.float32)
                value = wrap_pad(row[...], width) * coef[level, 5]
                for _ in range(ADV_STEPS):
                    value = (
                        coef[level, 0] * value
                        + coef[level, 1] * pltpu.roll(value, wide - 1, 2)
                        + coef[level, 2] * pltpu.roll(value, 1, 2)
                        + coef[level, 3] * pltpu.roll(value, lats - 1, 1)
                        + coef[level, 4] * pltpu.roll(value, 1, 1)
                    )
                start = pl.multiple_of((level * fields + first) * lats, FIELD_STEP * lats)
                value = value.reshape(FIELD_STEP * lats, wide)
                for tile in range(wide // LANES):
                    lanes = value[:, tile * LANES : (tile + 1) * LANES]
                    moved[tile, pl.ds(start, FIELD_STEP * lats)] = lanes
                return carry

            lax.fori_loop(0, fields // FIELD_STEP, body, 0)

    picked = pl.ds(step_id, levels * fields, stride=lats)
    source = [moved[tile, picked].astype(jnp.bfloat16) for tile in range(wide // LANES)]
    source = jnp.concatenate(source, axis=1)
    rank = rank_ref[0]
    for start in range(0, ROW_OCEAN, WIDE):
        slots = lax.broadcasted_iota(jnp.int32, (WIDE, wide), 0) + start
        pick = jnp.where(slots == rank, 1.0, 0.0).astype(jnp.bfloat16)
        packed = lax.dot_general(
            source, pick, (((1,), (1,)), ((), ())), preferred_element_type=jnp.float32
        )
        out_ref[0, :, :, :, start : start + WIDE] = packed.reshape(
            out_ref.shape[1:4] + (WIDE,)
        ).astype(jnp.bfloat16)


def transport_packed(tracer_state, velocity, land_mask, rank, tracers, chunk):
    fields, levels, lats, width = tracer_state.shape
    wide = rank.shape[-1]
    part = levels // CHUNKS
    return pl.pallas_call(
        transport_kernel,
        grid=(lats,),
        in_specs=[
            pl.BlockSpec((fields, part, lats, width), lambda k: (0, chunk, 0, 0)),
            pl.BlockSpec((2, part, lats, width), lambda k: (0, chunk, 0, 0)),
            pl.BlockSpec((lats, width), lambda k: (0, 0)),
            pl.BlockSpec((1, 1, wide), lambda k: (k, 0, 0)),
        ],
        out_specs=pl.BlockSpec(
            (1, part, fields // tracers, tracers, ROW_OCEAN), lambda k: (k, 0, 0, 0, 0)
        ),
        out_shape=jax.ShapeDtypeStruct(
            (lats, part, fields // tracers, tracers, ROW_OCEAN), jnp.bfloat16
        ),
        scratch_shapes=[
            pltpu.VMEM((part, 6, lats, wide), jnp.float32),
            pltpu.VMEM((FIELD_STEP, lats, wide), jnp.float32),
            pltpu.VMEM((lats, wide), jnp.float32),
            pltpu.VMEM((wide // LANES, part * fields * lats, LANES), jnp.float32),
        ],
        compiler_params=pltpu.CompilerParams(vmem_limit_bytes=48 * 1024 * 1024),
        cost_estimate=pl.CostEstimate(
            flops=2 * part * fields * lats * wide * ROW_OCEAN,
            bytes_accessed=4 * part * fields * lats * width,
            transcendentals=0,
        ),
        name="transport",
    )(tracer_state, velocity, land_mask, rank[:, None])


def half_silu(half):
    return (half + half * jnp.tanh(half)).astype(jnp.bfloat16)


def reaction_kernel(
    first_level,
    packed_ref,
    in_ref,
    bias_one_ref,
    hid_ref,
    bias_two_ref,
    coef_ref,
    rank_ref,
    cell_ref,
    *rest,
):
    out_ref, seen_ref, spread, fresh = rest[-4:]
    sources, _, per_source, tracers, slots = packed_ref.shape
    width = out_ref.shape[1]
    members = coef_ref.shape[0]
    hidden = hid_ref.shape[0]

    @pl.when(pl.program_id(0) == 0)
    def _():
        for start in range(0, slots, LANES):
            ids = lax.broadcasted_iota(jnp.int32, (width, LANES), 1) + start
            same = jnp.where(ids == rank_ref[...], 1.0, 0.0)
            spread[:, start : start + LANES] = same.astype(jnp.bfloat16)

    def body(index, carry):
        both = []
        for half in range(2):
            member = 2 * index + half
            source = lax.div(member, per_source)
            inner = lax.rem(member, per_source)
            parts = []
            for start in range(0, slots, WIDE):
                fields = packed_ref[source, 0, inner, :, start : start + WIDE]
                one = jnp.dot(in_ref[...], fields, preferred_element_type=jnp.float32)
                one = half_silu(one + bias_one_ref[...])
                two = jnp.dot(hid_ref[...], one, preferred_element_type=jnp.float32)
                two = half_silu(two + bias_two_ref[...])
                change = jnp.dot(coef_ref[member], two, preferred_element_type=jnp.float32)
                parts.append(fields.astype(jnp.float32) + change * hidden ** (-0.5))
            both.append(jnp.concatenate(parts, axis=1))
        pair = jnp.concatenate(both, axis=0).astype(jnp.bfloat16)
        fresh[pl.ds(pl.multiple_of(index * 2 * tracers, 16), 2 * tracers)] = pair
        return carry

    lax.fori_loop(0, members // 2, body, 0)
    cells = lax.dot_general(
        spread[...], fresh[...], (((1,), (1,)), ((), ())), preferred_element_type=jnp.float32
    ).astype(jnp.bfloat16)
    out_ref[0] = cells
    level = first_level + pl.program_id(0)
    ids = lax.broadcasted_iota(jnp.int32, (OBS_CAP, width), 1) + level * width
    pick = jnp.where(ids == cell_ref[...], 1.0, 0.0).astype(jnp.bfloat16)
    seen = jnp.dot(pick, cells, preferred_element_type=jnp.float32)

    @pl.when(pl.program_id(0) == 0)
    def _():
        seen_ref[...] = seen

    @pl.when(pl.program_id(0) > 0)
    def _():
        seen_ref[...] += seen


def reaction(
    packed, in_t, bias_one, hid_t, bias_two, coef_half, rank_own, obs_cell, levels, first, earlier
):
    sources, part, per_source, tracers, slots = packed.shape
    members, _, hidden = coef_half.shape
    width = rank_own.shape[0]
    rows = members * tracers
    whole = lambda *dims: pl.BlockSpec(dims, lambda level: (0,) * len(dims))
    return pl.pallas_call(
        functools.partial(reaction_kernel, first),
        grid=(part,),
        in_specs=[
            pl.BlockSpec(
                (sources, 1, per_source, tracers, slots), lambda level: (0, level, 0, 0, 0)
            ),
            whole(hidden, tracers),
            whole(hidden, 1),
            whole(hidden, hidden),
            whole(hidden, 1),
            whole(members, tracers, hidden),
            whole(*rank_own.shape),
            whole(OBS_CAP, 1),
        ]
        + [pl.BlockSpec(memory_space=pl.ANY)] * len(earlier),
        out_specs=[
            pl.BlockSpec((1, width, rows), lambda level: (first + level, 0, 0)),
            whole(OBS_CAP, rows),
        ],
        out_shape=[
            jax.ShapeDtypeStruct((levels, width, rows), jnp.bfloat16),
            jax.ShapeDtypeStruct((OBS_CAP, rows), jnp.float32),
        ],
        input_output_aliases={8: 0} if earlier else {},
        scratch_shapes=[
            pltpu.VMEM((width, slots), jnp.bfloat16),
            pltpu.VMEM((rows, slots), jnp.bfloat16),
        ],
        compiler_params=pltpu.CompilerParams(vmem_limit_bytes=48 * 1024 * 1024),
        cost_estimate=pl.CostEstimate(
            flops=2 * part * rows * slots * (width + 2 * hidden + hidden * hidden // tracers),
            bytes_accessed=2 * part * rows * (slots + width),
            transcendentals=2 * part * members * slots * hidden,
        ),
        name="reaction",
    )(packed, in_t, bias_one, hid_t, bias_two, coef_half, rank_own, obs_cell, *earlier)


def solve_system(system, right_side):
    factor = jnp.linalg.cholesky(system)
    middle = lax.linalg.triangular_solve(factor, right_side, left_side=True, lower=True)
    return lax.linalg.triangular_solve(factor, middle, left_side=True, lower=True, transpose_a=True)


def shards(
    tracer_state,
    velocity,
    land_mask,
    in_weight,
    bias_one,
    hid_weight,
    bias_two,
    out_coef,
    obs_cell,
    obs_count,
    obs_value,
    obs_var,
    obs_noise,
):
    own_block = lax.axis_index("trc")
    group_index = lax.axis_index("ens")
    field_rows, levels, lat_rows, lon_count = tracer_state.shape
    members_here = out_coef.shape[0]
    tracers = in_weight.shape[0]
    group_rows = members_here * tracers
    highest = lax.Precision.HIGHEST
    wide = -(-lon_count // LANES) * LANES
    below = jnp.arange(lon_count)[:, None] < jnp.arange(lon_count)[None, :]
    before = jnp.dot(
        land_mask.astype(jnp.bfloat16), below.astype(jnp.bfloat16), preferred_element_type=jnp.float32
    )
    rank = jnp.where(land_mask > 0, before.astype(jnp.int32), -1)
    rank = jnp.pad(rank, ((0, 0), (0, wide - lon_count)), constant_values=-1)
    rank_own = lax.dynamic_slice_in_dim(rank, own_block, 1, 0)[:, :lon_count].T
    coef_half = out_coef.astype(jnp.bfloat16)
    in_t = in_weight.T * jnp.bfloat16(0.5)
    hid_t = hid_weight.T * jnp.bfloat16(0.5)
    half_one = bias_one[:, None] * 0.5
    half_two = bias_two[:, None] * 0.5
    part = levels // CHUNKS
    received = []
    for chunk in range(CHUNKS):
        packed = transport_packed(tracer_state, velocity, land_mask, rank, tracers, chunk)
        received.append(lax.all_to_all(packed, "trc", split_axis=0, concat_axis=0, tiled=True))
    earlier = []
    predicted = 0.0
    for chunk in range(CHUNKS):
        cells, seen = reaction(
            received[chunk],
            in_t,
            half_one,
            hid_t,
            half_two,
            coef_half,
            rank_own,
            obs_cell.T,
            levels,
            chunk * part,
            earlier,
        )
        earlier = [cells]
        predicted = predicted + seen
    new_cols = jnp.transpose(earlier[0], (2, 0, 1))[:, :, None]
    predicted_own = predicted.T.reshape(members_here, tracers, OBS_CAP)[:, :OBS_TR]
    predicted_own = predicted_own.astype(jnp.bfloat16)
    predicted_all = lax.all_gather(predicted_own, "ens", axis=0, tiled=True)
    member_total = predicted_all.shape[0]
    slot_ids = jnp.arange(OBS_CAP, dtype=jnp.int32)
    valid_slots = (slot_ids < obs_count[0]).astype(jnp.float32)
    weight = valid_slots[None, :] / obs_var[0]
    guessed = predicted_all.astype(jnp.float32).reshape(member_total, -1)
    anomaly = guessed - jnp.mean(guessed, axis=0)
    misfit = (obs_value[None] + obs_noise).reshape(member_total, -1) - guessed
    weighted = anomaly * weight.reshape(1, -1)
    terms = jnp.dot(
        weighted,
        jnp.concatenate([anomaly, misfit], axis=0).T,
        precision=highest,
        preferred_element_type=jnp.float32,
    )
    terms = jnp.sum(lax.all_gather(terms, "trc", axis=0), axis=0)
    gram, cross = terms[:, :member_total], terms[:, member_total:]
    system = (member_total - 1) * jnp.eye(member_total, dtype=jnp.float32) + gram
    mixing = solve_system(system, cross)
    flat_coef = out_coef.reshape(members_here, -1)
    first_member = group_index * members_here
    mixing_rows = lax.dynamic_slice_in_dim(mixing, first_member, members_here, 0)
    summed = lax.psum_scatter(
        jnp.dot(mixing_rows.T, flat_coef, precision=highest, preferred_element_type=jnp.float32),
        "ens",
        scatter_dimension=0,
        tiled=True,
    )
    new_coef = flat_coef + summed
    return (new_cols, new_coef.reshape(members_here, tracers, -1))


def solution(mesh):
    in_specs = (
        P(("ens", "trc"), None, None, None),
        P(),
        P(),
        P(),
        P(),
        P(),
        P(),
        P("ens", None, None),
        P("trc", None),
        P("trc"),
        P("trc", None, None),
        P("trc", None, None),
        P(None, "trc", None, None),
    )
    out_specs = (P("ens", None, "trc", None), P("ens", None, None))
    return jax.shard_map(shards, mesh=mesh, in_specs=in_specs, out_specs=out_specs, check_vma=False)
```

time: 602 us -> 304 us (0.50)
  local copies, waits for them, and re-layouts: 197 us -> 25.3 us
  matrix products: 143 us -> 4.98 us
  Pallas kernels: 0 us -> 138 us
  other arithmetic: 81.2 us -> 21.3 us
  waiting for transfers between devices: 110 us -> 50.2 us
    dot_general x34 -> x2, matrix products: 140 us -> 1.94 us  [the longest x1 1.41 us: shards(): jnp.dot(land_mask.astype(jnp.bfloat16), below.astype(jnp.bfloat16), prefe...]
    pallas_call x0 -> x4, Pallas kernels: none -> 138 us  [the longest x2 99.3 us: reaction(): pl.pallas_call(functools.partial(reaction_kernel, first), grid=(part,), i...]
    gather x3 -> x0, local copies, waits for them, and re-layouts: 116 us -> none  [shards(): predicted_own = jnp.take_along_axis(observed, cell_index, axis=2)]
    all_to_all x1 -> x2, waiting for transfers between devices: 103 us -> 21 us  [shards(): lax.all_to_all(packed, 'trc', split_axis=0, concat_axis=0, tiled=True)]
    slice x14 -> x2, local copies, waits for them, and re-layouts: 40 us -> 0.01 us  [shards(): predicted.T.reshape(members_here, tracers, OBS_CAP)[:, :OBS_TR]]
    psum x1 -> x0, blocking collectives: 35.7 us -> none  [shards(): gram, cross = lax.psum((gram_part, cross_part), 'trc')]
    all_gather x0 -> x1, blocking collectives: none -> 31.3 us  [shards(): terms = jnp.sum(lax.all_gather(terms, 'trc', axis=0), axis=0)]
    add x3 -> x1, other arithmetic: 30.9 us -> 2.16 us  [shards(): misfit = (obs_value[None] + obs_noise).reshape(member_total, -1) - guessed]
  transfers between devices with their start and end apart: 2 -> 3, of which waited for: 2 -> 2; matrix products, arithmetic and copies ran while one was open for 3% -> 6% of each run, Pallas kernels for 0% -> 23%
where the time goes in v1:
time: 304 us; the launch traced here: 302 us
  Pallas kernels  138 us (45%)
  waiting for transfers between devices  50.2 us (17%)
  blocking collectives  36.9 us (12%)
  local copies, waits for them, and re-layouts  25.3 us (8%)
  other arithmetic  21.3 us (7%)
  between operations  14.9 us (5%)
  starting transfers between devices  10.9 us (4%)
  matrix products  4.98 us (2%)
    pallas_call x2, Pallas kernels, reaction(): pl.pallas_call(functools.partial(reaction_kernel, first), grid=(part,), i...  99.3 us
    pallas_call x2, Pallas kernels, transport_packed(): pl.pallas_call(transport_kernel, grid=(lats,), in_specs=[pl.BlockSpec((fi...  38.8 us
    all_gather x1, blocking collectives, shards(): terms = jnp.sum(lax.all_gather(terms, 'trc', axis=0), axis=0)  31.3 us
    reduce_scatter x1, waiting for transfers between devices, shards(): lax.psum_scatter(jnp.dot(mixing_rows.T, flat_coef, precision=highest, pre...  29.1 us
    all_to_all x2, waiting for transfers between devices, shards(): lax.all_to_all(packed, 'trc', split_axis=0, concat_axis=0, tiled=True)  21 us
    unnamed x51, local copies, waits for them, and re-layouts  20.1 us
    all_to_all x2, starting transfers between devices, shards(): lax.all_to_all(packed, 'trc', split_axis=0, concat_axis=0, tiled=True)  10.9 us
    another operation x3, other arithmetic, solve_system(): factor = jnp.linalg.cholesky(system)  6.54 us
  transfers between devices with their start and end apart: 3, of which 2 were waited for; matrix products, arithmetic and copies ran while one was open for 6% of the time, Pallas kernels for 23%

profile of v1, /device:TPU:0, one launch (start us, length us, event | category | flops | bytes accessed | tf_op | source)
XLA Modules:
  0.0 302.4 jit_solution(2812148081237460327)
XLA Ops:
  7.2 1.4 fusion.3
  9.3 19.8 %transport.3 = bf16[8,2,2,24,1152]{4,3,2,1,0:T(8,128)(2,1)} custom-call(bf16[48,4,8,1440]{3,2,1,0:T(8,128)(2,1)} %state_ref.3, f32[2,4,8,1440]{3,2,1,0:T(8,128)S(1)} %copy-done.17, s32[8,1440]{1,0:T(8,128)S(1)} %copy-done.18, s32[8,1,1536]{2,1,0:T(1,128)S(1)} %broadcast_in_dim.10.rank_ref), custom_call_target="tpu_custom_call" | custom-call | flops 2717908992 | bytes 4423680 | tf_op jit(solution)/shard_map/transport/pallas_call | solution.py:105
  29.0 7.3 %all-to-all-start.1 = ((bf16[8,2,2,24,1152]{4,3,2,1,0:T(8,128)(2,1)}), bf16[8,2,2,24,1152]{4,3,2,1,0:T(8,128)(2,1)S(1)}, u32[]{:S(2)}, u32[]{:S(2)}) async-start(bf16[8,2,2,24,1152]{4,3,2,1,0:T(8,128)(2,1)} %transport.3), calls=%async_computation.1 | async-start | bytes 3538944 | tf_op jit(solution)/shard_map/all_to_all | solution.py:296
  36.3 19.0 %transport.2 = bf16[8,2,2,24,1152]{4,3,2,1,0:T(8,128)(2,1)S(1)} custom-call(bf16[48,4,8,1440]{3,2,1,0:T(8,128)(2,1)} %state_ref.3, f32[2,4,8,1440]{3,2,1,0:T(8,128)S(1)} %copy-done.17, s32[8,1440]{1,0:T(8,128)S(1)} %copy-done.18, s32[8,1,1536]{2,1,0:T(1,128)S(1)} %broadcast_in_dim.10.rank_ref), custom_call_target="tpu_custom_call" | custom-call | flops 2717908992 | bytes 4423680 | tf_op jit(solution)/shard_map/transport/pallas_call | solution.py:105
  55.3 1.2 copy-done
  56.5 21.0 %all-to-all-done.1.packed_ref = bf16[8,2,2,24,1152]{4,3,2,1,0:T(8,128)(2,1)S(1)} async-done(((bf16[8,2,2,24,1152]{4,3,2,1,0:T(8,128)(2,1)}), bf16[8,2,2,24,1152]{4,3,2,1,0:T(8,128)(2,1)S(1)}, u32[]{:S(2)}, u32[]{:S(2)}) %all-to-all-start.1) | async-done | bytes 1769504 | tf_op jit(solution)/shard_map/all_to_all | solution.py:296
  77.5 3.6 %all-to-all-start = ((bf16[8,2,2,24,1152]{4,3,2,1,0:T(8,128)(2,1)}), bf16[8,2,2,24,1152]{4,3,2,1,0:T(8,128)(2,1)S(1)}, u32[]{:S(2)}, u32[]{:S(2)}) async-start(bf16[8,2,2,24,1152]{4,3,2,1,0:T(8,128)(2,1)} %copy-done), calls=%async_computation | async-start | bytes 3538944 | tf_op jit(solution)/shard_map/all_to_all | solution.py:296
  82.0 1.2 copy.59.rank_ref
  83.2 1.7 copy.52
  84.8 1.7 convert_element_type.28.coef_ref
  89.5 1.4 copy.50
  90.9 1.4 copy.60.cell_ref
  92.9 1.9 copy.68
  94.8 2.2 add_reduce_fusion
  98.8 1.1 copy-done.1
  103.5 49.6 %reaction.2 = (bf16[4,1440,384]{2,1,0:T(8,128)(2,1)}, f32[128,384]{1,0:T(8,128)S(1)}) custom-call(bf16[8,2,2,24,1152]{4,3,2,1,0:T(8,128)(2,1)S(1)} %all-to-all-done.1.packed_ref, bf16[256,24]{1,0:T(8,128)(2,1)S(1)} %multiply_bitcast_fusion.1.in_ref, f32[256,1]{1,0:T(8,128)S(1)} %copy-done.7, bf16[256,256]{1,0:T(8,128)(2,1)S(1)} %multiply_bitcast_fusion.hid_ref, ...), custom_call_target="tpu_custom_call" | custom-call | flops 8284667904 | bytes 3981312 | tf_op jit(solution)/shard_map/reaction/pallas_call | solution.py:212
  154.5 1.1 copy-done.2
  160.9 49.6 %reaction.3 = (bf16[4,1440,384]{2,1,0:T(8,128)(2,1)}, f32[128,384]{1,0:T(8,128)S(1)}) custom-call(bf16[8,2,2,24,1152]{4,3,2,1,0:T(8,128)(2,1)S(1)} %all-to-all-done.packed_ref, bf16[256,24]{1,0:T(8,128)(2,1)S(1)} %copy-done.16, f32[256,1]{1,0:T(8,128)S(1)} %copy-done.8, bf16[256,256]{1,0:T(8,128)(2,1)S(1)} %copy-done.12, ...), custom_call_target="tpu_custom_call", output_to_operand_aliasing={{0}: (8, {})} | custom-call | flops 8284667904 | bytes 3981312 | tf_op jit(solution)/shard_map/reaction/pallas_call | solution.py:212
  210.7 5.6 %all_gather.9 = bf16[64,6,128]{2,0,1:T(8,128)(2,1)S(1)} all-gather(bf16[16,6,128]{2,0,1:T(8,128)(2,1)S(1)} %copy.62), channel_id=1, replica_groups=mesh['ens'=4,'trc'=8] {'ens'}, dimensions={0}, use_global_device_ids=true | all-gather | bytes 122880 | tf_op jit(solution)/shard_map/all_gather | solution.py:318
  217.9 31.3 %all-gather = f32[512,128]{1,0:T(8,128)S(1)} all-gather(f32[64,128]{1,0:T(8,128)S(1)} %fusion.4), channel_id=2, replica_groups=mesh['ens'=4,'trc'=8] {'trc'}, dimensions={0}, use_global_device_ids=true | all-gather | bytes 294912 | tf_op jit(solution)/shard_map/all_gather | solution.py:333
  249.3 5.8 %cholesky.16 = f32[64,64]{1,0:T(8,128)S(1)} custom-call(f32[64,64]{1,0:T(8,128)S(1)} %fusion.17), custom_call_target="Cholesky" | custom-call | tf_op jit(solution)/shard_map/jit(cholesky)/cholesky | solution.py:252
  256.5 4.9 %custom-call.8 = f32[1,64,64]{1,2,0:T(8,128)S(1)} custom-call(f32[1,64,64]{2,1,0:T(8,128)S(1)} %fusion.11), custom_call_target="InvertDiagBlocksLowerTriangular" | custom-call | tf_op jit(solution)/shard_map/triangular_solve | solution.py:254
  261.9 2.6 fusion.19
  264.5 29.1 %reduce-scatter.2.cloned.1.call-done = f32[16,6144]{1,0:T(8,128)} async-done(((f32[64,6144]{1,0:T(8,128)}), f32[16,6144]{1,0:T(8,128)}) %reduce-scatter.2.cloned.1.call-update) | async-done | bytes 393232 | tf_op jit(solution)/shard_map/reduce_scatter | solution.py:340
  (78 shorter events, 22.0 us)
Async XLA Ops:
  7.2 2.1 copy-start.18
  7.2 2.1 copy-start.17
  29.0 48.5 %all-to-all-start.1 = ((bf16[8,2,2,24,1152]{4,3,2,1,0:T(8,128)(2,1)}), bf16[8,2,2,24,1152]{4,3,2,1,0:T(8,128)(2,1)S(1)}, u32[]{:S(2)}, u32[]{:S(2)}) async-start(bf16[8,2,2,24,1152]{4,3,2,1,0:T(8,128)(2,1)} %transport.3), calls=%async_computation.1 | async-start | bytes 3538944 | tf_op jit(solution)/shard_map/all_to_all | solution.py:296
  55.3 1.2 copy-start
  56.5 35.8 %copy-start.21 = (f32[1,6,128]{2,0,1:T(1,128)S(1)}, f32[1,6,128]{2,0,1:T(1,128)}, u32[]{:S(2)}) copy-start(f32[1,6,128]{2,0,1:T(1,128)} %param.23) | copy-start | bytes 9220
  77.5 77.0 %all-to-all-start = ((bf16[8,2,2,24,1152]{4,3,2,1,0:T(8,128)(2,1)}), bf16[8,2,2,24,1152]{4,3,2,1,0:T(8,128)(2,1)S(1)}, u32[]{:S(2)}, u32[]{:S(2)}) async-start(bf16[8,2,2,24,1152]{4,3,2,1,0:T(8,128)(2,1)} %copy-done), calls=%async_computation | async-start | bytes 3538944 | tf_op jit(solution)/shard_map/all_to_all | solution.py:296
  81.1 13.7 %copy-start.22 = (f32[1,6,128]{2,0,1:T(1,128)S(1)}, f32[1,6,128]{2,0,1:T(1,128)}, u32[]{:S(2)}) copy-start(f32[1,6,128]{2,0,1:T(1,128)} %param.24) | copy-start | bytes 9220
  81.1 212.5 %reduce-scatter.2.cloned.1.call-start = ((), (), s32[]{:S(2)}) async-start(), calls=%async_computation.3 | async-start | bytes 1966080 | tf_op jit(solution)/shard_map/reduce_scatter | solution.py:340
  97.9 1.0 copy-start.15
  98.8 1.1 copy-start.1
  99.9 0.9 copy-start.3
  100.9 0.9 copy-start.7
  101.8 0.9 copy-start.9
  102.7 0.8 copy-start.13
  153.1 0.7 copy-start.5
  154.5 1.1 copy-start.2
  155.6 0.9 copy-start.4
  156.5 0.9 copy-start.8
  157.4 0.9 copy-start.10
  158.3 0.9 copy-start.12
  159.2 0.8 copy-start.14
  160.1 0.8 copy-start.16
  160.9 49.7 %copy-start.6 = (f32[128,384]{1,0:T(8,128)S(1)}, f32[128,384]{1,0:T(8,128)}, u32[]{:S(2)}) copy-start(f32[128,384]{1,0:T(8,128)} %copy-done.5) | copy-start | bytes 589828
  210.6 51.3 %copy-start.19 = (f32[2,8,24,256]{3,1,2,0:T(8,128)S(1)}, f32[2,8,24,256]{3,1,2,0:T(8,128)}, u32[]{:S(2)}) copy-start(f32[2,8,24,256]{3,1,2,0:T(8,128)} %copy.68) | copy-start | bytes 1179652
  (2 other events, 1.3 us)
Sparse Core Ops, SparseCore 0:
  264.6 28.9 reduce-scatter.1

commit v2 on v1

--- a/solution.py
+++ b/solution.py
@@ -134,7 +134,8 @@
 
 
 def half_silu(half):
-    return (half + half * jnp.tanh(half)).astype(jnp.bfloat16)
+    half = half.astype(jnp.bfloat16)
+    return half * (jnp.tanh(half) + jnp.bfloat16(1.0))
 
 
 def reaction_kernel(
@@ -246,6 +247,55 @@
         ),
         name="reaction",
     )(packed, in_t, bias_one, hid_t, bias_two, coef_half, rank_own, obs_cell, *earlier)
+
+
+def sum_kernel(count, term_ref, out_ref, slots, send_sem, recv_sem):
+    own = lax.axis_index("trc")
+    peers = [lax.rem(own + step, count) for step in range(1, count)]
+    barrier = pltpu.get_barrier_semaphore()
+    for peer in peers:
+        pl.semaphore_signal(
+            barrier, inc=1, device_id={"trc": peer}, device_id_type=pl.DeviceIdType.MESH
+        )
+    pl.semaphore_wait(barrier, count - 1)
+    copies = []
+    for step, peer in enumerate(peers):
+        copy = pltpu.make_async_remote_copy(
+            src_ref=term_ref,
+            dst_ref=slots.at[own],
+            send_sem=send_sem.at[step],
+            recv_sem=recv_sem.at[step],
+            device_id={"trc": peer},
+            device_id_type=pl.DeviceIdType.MESH,
+        )
+        copy.start()
+        copies.append(copy)
+    slots[own] = term_ref[...]
+    for copy in copies:
+        copy.wait()
+    total = slots[0]
+    for source in range(1, count):
+        total = total + slots[source]
+    out_ref[...] = total
+
+
+def sum_over_blocks(terms):
+    count = lax.axis_size("trc")
+    return pl.pallas_call(
+        functools.partial(sum_kernel, count),
+        in_specs=[pl.BlockSpec(memory_space=pltpu.VMEM)],
+        out_specs=pl.BlockSpec(memory_space=pltpu.VMEM),
+        out_shape=jax.ShapeDtypeStruct(terms.shape, terms.dtype),
+        scratch_shapes=[
+            pltpu.VMEM((count,) + terms.shape, terms.dtype),
+            pltpu.SemaphoreType.DMA((count - 1,)),
+            pltpu.SemaphoreType.DMA((count - 1,)),
+        ],
+        compiler_params=pltpu.CompilerParams(
+            collective_id=0, has_side_effects=True, vmem_limit_bytes=16 * 1024 * 1024
+        ),
+        name="block_sum",
+    )(terms)
 
 
 def solve_system(system, right_side):
@@ -289,9 +339,17 @@
     hid_t = hid_weight.T * jnp.bfloat16(0.5)
     half_one = bias_one[:, None] * 0.5
     half_two = bias_two[:, None] * 0.5
+    flat_coef = out_coef.reshape(members_here, -1)
+    coef_all = lax.all_gather(flat_coef, "ens", axis=0, tiled=True)
+    obs_own = (obs_value[None] + obs_noise).reshape(obs_noise.shape[0], -1)
+    cell_column = obs_cell.T
     part = levels // CHUNKS
     received = []
     for chunk in range(CHUNKS):
+        if chunk == 1:
+            ready = (rank, rank_own, coef_half, in_t, hid_t, half_one, half_two, cell_column, obs_own)
+            ready = lax.optimization_barrier(ready)
+            rank, rank_own, coef_half, in_t, hid_t, half_one, half_two, cell_column, obs_own = ready
         packed = transport_packed(tracer_state, velocity, land_mask, rank, tracers, chunk)
         received.append(lax.all_to_all(packed, "trc", split_axis=0, concat_axis=0, tiled=True))
     earlier = []
@@ -305,7 +363,7 @@
             half_two,
             coef_half,
             rank_own,
-            obs_cell.T,
+            cell_column,
             levels,
             chunk * part,
             earlier,
@@ -322,7 +380,7 @@
     weight = valid_slots[None, :] / obs_var[0]
     guessed = predicted_all.astype(jnp.float32).reshape(member_total, -1)
     anomaly = guessed - jnp.mean(guessed, axis=0)
-    misfit = (obs_value[None] + obs_noise).reshape(member_total, -1) - guessed
+    misfit = obs_own - guessed
     weighted = anomaly * weight.reshape(1, -1)
     terms = jnp.dot(
         weighted,
@@ -330,18 +388,14 @@
         precision=highest,
         preferred_element_type=jnp.float32,
     )
-    terms = jnp.sum(lax.all_gather(terms, "trc", axis=0), axis=0)
+    terms = sum_over_blocks(terms)
     gram, cross = terms[:, :member_total], terms[:, member_total:]
     system = (member_total - 1) * jnp.eye(member_total, dtype=jnp.float32) + gram
     mixing = solve_system(system, cross)
-    flat_coef = out_coef.reshape(members_here, -1)
     first_member = group_index * members_here
-    mixing_rows = lax.dynamic_slice_in_dim(mixing, first_member, members_here, 0)
-    summed = lax.psum_scatter(
-        jnp.dot(mixing_rows.T, flat_coef, precision=highest, preferred_element_type=jnp.float32),
-        "ens",
-        scatter_dimension=0,
-        tiled=True,
+    mixing_own = lax.dynamic_slice_in_dim(mixing, first_member, members_here, 1)
+    summed = jnp.dot(
+        mixing_own.T, coef_all, precision=highest, preferred_element_type=jnp.float32
     )
     new_coef = flat_coef + summed
     return (new_cols, new_coef.reshape(members_here, tracers, -1))

time: 304 us -> 242 us (0.80)
  waiting for transfers between devices: 50.2 us -> 17.3 us
  blocking collectives: 36.9 us -> 5.56 us
  Pallas kernels: 138 us -> 148 us
  other arithmetic: 21.3 us -> 16.4 us
    all_gather x1 -> x0, blocking collectives: 31.3 us -> none  [shards(): terms = jnp.sum(lax.all_gather(terms, 'trc', axis=0), axis=0)]
    reduce_scatter x1 -> x0, waiting for transfers between devices: 29.1 us -> none  [shards(): lax.psum_scatter(jnp.dot(mixing_rows.T, flat_coef, precision=highest, pre...]
    pallas_call x0 -> x1, Pallas kernels: none -> 10.1 us  [sum_over_blocks(): pl.pallas_call(functools.partial(sum_kernel, count), in_specs=[pl.BlockSp...]
    optimization_barrier x0 -> x4, local copies, waits for them, and re-layouts: none -> 4.14 us  [shards(): ready = lax.optimization_barrier(ready)]
    all_to_all x2, waiting for transfers between devices: 21 us -> 17.3 us  [shards(): lax.all_to_all(packed, 'trc', split_axis=0, concat_axis=0, tiled=True)]
    unnamed x51 -> x60, local copies, waits for them, and re-layouts: 20.1 us -> 18.5 us
  transfers between devices with their start and end apart: 3 -> 3, of which waited for: 2 -> 1; matrix products, arithmetic and copies ran while one was open for 6% -> 10% of each run, Pallas kernels for 23% -> 53%
where the time goes in v2:
time: 242 us; the launch traced here: 241 us
  Pallas kernels  148 us (61%)
  local copies, waits for them, and re-layouts  23 us (10%)
  waiting for transfers between devices  17.3 us (7%)
  other arithmetic  16.4 us (7%)
  between operations  15 us (6%)
  starting transfers between devices  11.1 us (5%)
  blocking collectives  5.56 us (2%)
  matrix products  4.73 us (2%)
    pallas_call x2, Pallas kernels, reaction(): pl.pallas_call(functools.partial(reaction_kernel, first), grid=(part,), i...  99.5 us
    pallas_call x2, Pallas kernels, transport_packed(): pl.pallas_call(transport_kernel, grid=(lats,), in_specs=[pl.BlockSpec((fi...  38.8 us
    unnamed x60, local copies, waits for them, and re-layouts  18.5 us
    all_to_all x2, waiting for transfers between devices, shards(): lax.all_to_all(packed, 'trc', split_axis=0, concat_axis=0, tiled=True)  17.3 us
    all_to_all x2, starting transfers between devices, shards(): lax.all_to_all(packed, 'trc', split_axis=0, concat_axis=0, tiled=True)  11 us
    pallas_call x1, Pallas kernels, sum_over_blocks(): pl.pallas_call(functools.partial(sum_kernel, count), in_specs=[pl.BlockSp...  10.1 us
    another operation x3, other arithmetic, solve_system(): factor = jnp.linalg.cholesky(system)  6.55 us
    all_gather x1, blocking collectives, shards(): predicted_all = lax.all_gather(predicted_own, 'ens', axis=0, tiled=True)  5.56 us
  transfers between devices with their start and end apart: 3, of which 1 were waited for; matrix products, arithmetic and copies ran while one was open for 10% of the time, Pallas kernels for 53%

profile of v2, /device:TPU:0, one launch (start us, length us, event | category | flops | bytes accessed | tf_op | source)
XLA Modules:
  0.0 241.4 jit_solution(15397881096158329307)
XLA Ops:
  7.2 1.4 fusion.3
  8.7 19.8 %transport.3 = bf16[8,2,2,24,1152]{4,3,2,1,0:T(8,128)(2,1)} custom-call(bf16[48,4,8,1440]{3,2,1,0:T(8,128)(2,1)} %state_ref.3, f32[2,4,8,1440]{3,2,1,0:T(8,128)S(1)} %copy-done.17, s32[8,1440]{1,0:T(8,128)S(1)} %copy-done.18, s32[8,1,1536]{2,1,0:T(1,128)S(1)} %broadcast_in_dim.24.rank_ref), custom_call_target="tpu_custom_call" | custom-call | flops 2717908992 | bytes 4423680 | tf_op jit(solution)/shard_map/transport/pallas_call | solution.py:105
  28.4 7.4 %all-to-all-start.1 = ((bf16[8,2,2,24,1152]{4,3,2,1,0:T(8,128)(2,1)}), bf16[8,2,2,24,1152]{4,3,2,1,0:T(8,128)(2,1)S(1)}, u32[]{:S(2)}, u32[]{:S(2)}) async-start(bf16[8,2,2,24,1152]{4,3,2,1,0:T(8,128)(2,1)} %transport.3), calls=%async_computation.1 | async-start | bytes 3538944 | tf_op jit(solution)/shard_map/all_to_all | solution.py:354
  39.5 19.0 %transport.2 = bf16[8,2,2,24,1152]{4,3,2,1,0:T(8,128)(2,1)S(1)} custom-call(bf16[48,4,8,1440]{3,2,1,0:T(8,128)(2,1)} %state_ref.3, f32[2,4,8,1440]{3,2,1,0:T(8,128)S(1)} %copy-done.17, s32[8,1440]{1,0:T(8,128)S(1)} %copy-done.18, s32[8,1,1536]{2,1,0:T(1,128)S(1)} %copy.56.rank_ref), custom_call_target="tpu_custom_call" | custom-call | flops 2717908992 | bytes 4423680 | tf_op jit(solution)/shard_map/transport/pallas_call | solution.py:105
  58.5 1.2 copy-done
  59.8 17.3 %all-to-all-done.1.packed_ref = bf16[8,2,2,24,1152]{4,3,2,1,0:T(8,128)(2,1)S(1)} async-done(((bf16[8,2,2,24,1152]{4,3,2,1,0:T(8,128)(2,1)}), bf16[8,2,2,24,1152]{4,3,2,1,0:T(8,128)(2,1)S(1)}, u32[]{:S(2)}, u32[]{:S(2)}) %all-to-all-start.1) | async-done | bytes 1769504 | tf_op jit(solution)/shard_map/all_to_all | solution.py:354
  77.1 3.6 %all-to-all-start = ((bf16[8,2,2,24,1152]{4,3,2,1,0:T(8,128)(2,1)}), bf16[8,2,2,24,1152]{4,3,2,1,0:T(8,128)(2,1)S(1)}, u32[]{:S(2)}, u32[]{:S(2)}) async-start(bf16[8,2,2,24,1152]{4,3,2,1,0:T(8,128)(2,1)} %copy-done), calls=%async_computation | async-start | bytes 3538944 | tf_op jit(solution)/shard_map/all_to_all | solution.py:354
  80.7 1.9 copy.73
  82.6 1.2 copy.63.rank_ref
  85.4 1.4 copy.64.cell_ref
  88.2 1.1 copy-done.1
  89.3 0.9 copy-done.3
  90.2 0.9 copy-done.7
  91.1 0.9 copy-done.9
  94.6 49.8 %reaction.2 = (bf16[4,1440,384]{2,1,0:T(8,128)(2,1)}, f32[128,384]{1,0:T(8,128)S(1)}) custom-call(bf16[8,2,2,24,1152]{4,3,2,1,0:T(8,128)(2,1)S(1)} %all-to-all-done.1.packed_ref, bf16[256,24]{1,0:T(8,128)(2,1)S(1)} %copy-done.13, f32[256,1]{1,0:T(8,128)S(1)} %copy-done.9, bf16[256,256]{1,0:T(8,128)(2,1)S(1)} %copy-done.7, f32[256,1]{1,0:T(8,128)S(1)} %copy-done.11, ...), custom_call_target="tpu_custom_call" | custom-call | flops 8284667904 | bytes 3981312 | tf_op jit(solution)/shard_map/reaction/pallas_call | solution.py:213
  145.1 1.1 copy-done.2
  146.2 0.9 copy-done.4
  151.5 49.8 %reaction.3 = (bf16[4,1440,384]{2,1,0:T(8,128)(2,1)}, f32[128,384]{1,0:T(8,128)S(1)}) custom-call(bf16[8,2,2,24,1152]{4,3,2,1,0:T(8,128)(2,1)S(1)} %all-to-all-done.packed_ref, bf16[256,24]{1,0:T(8,128)(2,1)S(1)} %copy-done.14, f32[256,1]{1,0:T(8,128)S(1)} %copy-done.10, bf16[256,256]{1,0:T(8,128)(2,1)S(1)} %copy-done.8, ...), custom_call_target="tpu_custom_call", output_to_operand_aliasing={{0}: (8, {})} | custom-call | flops 8284667904 | bytes 3981312 | tf_op jit(solution)/shard_map/reaction/pallas_call | solution.py:213
  201.5 5.6 %all_gather.6 = bf16[64,6,128]{2,0,1:T(8,128)(2,1)S(1)} all-gather(bf16[16,6,128]{2,0,1:T(8,128)(2,1)S(1)} %copy.66), channel_id=1, replica_groups=mesh['ens'=4,'trc'=8] {'ens'}, dimensions={0}, use_global_device_ids=true | all-gather | bytes 122880 | tf_op jit(solution)/shard_map/all_gather | solution.py:376
  207.1 1.0 bitcast_subtract_fusion.1
  208.6 10.1 %block_sum.1 = f32[64,128]{1,0:T(8,128)S(1)} custom-call(f32[64,128]{1,0:T(8,128)S(1)} %fusion.4.term_ref), custom_call_target="tpu_custom_call" | custom-call | tf_op jit(solution)/shard_map/block_sum/pallas_call | solution.py:284
  218.8 5.8 %cholesky.16 = f32[64,64]{1,0:T(8,128)S(1)} custom-call(f32[64,64]{1,0:T(8,128)S(1)} %fusion.16), custom_call_target="Cholesky" | custom-call | tf_op jit(solution)/shard_map/jit(cholesky)/cholesky | solution.py:302
  226.0 4.9 %custom-call.8 = f32[1,64,64]{1,2,0:T(8,128)S(1)} custom-call(f32[1,64,64]{2,1,0:T(8,128)S(1)} %fusion.11), custom_call_target="InvertDiagBlocksLowerTriangular" | custom-call | tf_op jit(solution)/shard_map/triangular_solve | solution.py:304
  231.4 2.3 convolution_add_fusion
  (86 shorter events, 17.2 us)
Async XLA Ops:
  7.2 1.5 copy-start.18
  7.2 1.5 copy-start.17
  28.4 7.4 %copy-start.24 = (f32[1,6,128]{2,0,1:T(1,128)S(1)}, f32[1,6,128]{2,0,1:T(1,128)}, u32[]{:S(2)}) copy-start(f32[1,6,128]{2,0,1:T(1,128)} %param.23) | copy-start | bytes 9220
  28.4 7.5 %copy-start.21 = (f32[64,1,6,128]{3,1,2,0:T(1,128)S(1)}, f32[64,1,6,128]{3,1,2,0:T(1,128)}, u32[]{:S(2)}) copy-start(f32[64,1,6,128]{3,1,2,0:T(1,128)} %param.25) | copy-start | bytes 589828
  28.4 8.7 %copy-start.22 = (bf16[256,256]{1,0:T(8,128)(2,1)S(1)}, bf16[256,256]{1,0:T(8,128)(2,1)}, u32[]{:S(2)}) copy-start(bf16[256,256]{1,0:T(8,128)(2,1)} %param.18) | copy-start | bytes 393220
  28.4 8.8 %copy-start.20 = (f32[16,24,256]{2,1,0:T(8,128)S(1)}, f32[16,24,256]{2,1,0:T(8,128)}, u32[]{:S(2)}) copy-start(f32[16,24,256]{2,1,0:T(8,128)} %param.20) | copy-start | bytes 1179652
  28.4 48.6 %all-to-all-start.1 = ((bf16[8,2,2,24,1152]{4,3,2,1,0:T(8,128)(2,1)}), bf16[8,2,2,24,1152]{4,3,2,1,0:T(8,128)(2,1)S(1)}, u32[]{:S(2)}, u32[]{:S(2)}) async-start(bf16[8,2,2,24,1152]{4,3,2,1,0:T(8,128)(2,1)} %transport.3), calls=%async_computation.1 | async-start | bytes 3538944 | tf_op jit(solution)/shard_map/all_to_all | solution.py:354
  35.8 2.1 copy-start.23
  35.8 2.3 copy-start.25
  35.9 2.3 copy-start.26
  58.5 1.2 copy-start
  77.1 68.0 %all-to-all-start = ((bf16[8,2,2,24,1152]{4,3,2,1,0:T(8,128)(2,1)}), bf16[8,2,2,24,1152]{4,3,2,1,0:T(8,128)(2,1)S(1)}, u32[]{:S(2)}, u32[]{:S(2)}) async-start(bf16[8,2,2,24,1152]{4,3,2,1,0:T(8,128)(2,1)} %copy-done), calls=%async_computation | async-start | bytes 3538944 | tf_op jit(solution)/shard_map/all_to_all | solution.py:354
  80.7 150.7 %all-gather.2.cloned.1.call-start = ((), (), s32[]{:S(2)}) async-start(), calls=%async_computation.2 | async-start | bytes 1966080 | tf_op jit(solution)/shard_map/all_gather | solution.py:343
  88.1 1.1 copy-start.1
  89.3 0.9 copy-start.3
  90.2 0.9 copy-start.7
  91.1 0.9 copy-start.9
  92.0 0.9 copy-start.11
  145.1 1.1 copy-start.2
  146.2 0.9 copy-start.4
  147.1 0.9 copy-start.8
  148.9 0.9 copy-start.12
  151.5 49.8 %copy-start.6 = (f32[128,384]{1,0:T(8,128)S(1)}, f32[128,384]{1,0:T(8,128)}, u32[]{:S(2)}) copy-start(f32[128,384]{1,0:T(8,128)} %copy-done.5) | copy-start | bytes 589828
  201.3 30.1 %copy-start.19 = (f32[2,8,24,256]{3,1,2,0:T(8,128)S(1)}, f32[2,8,24,256]{3,1,2,0:T(8,128)}, u32[]{:S(2)}) copy-start(f32[2,8,24,256]{3,1,2,0:T(8,128)} %copy.73) | copy-start | bytes 1179652
  (6 other events, 4.9 us)
Sparse Core Ops, SparseCore 0:
  83.7 21.0 all-gather.1

commit v3 on v2

--- a/solution.py
+++ b/solution.py
@@ -134,8 +134,7 @@
 
 
 def half_silu(half):
-    half = half.astype(jnp.bfloat16)
-    return half * (jnp.tanh(half) + jnp.bfloat16(1.0))
+    return (half + half * jnp.tanh(half)).astype(jnp.bfloat16)
 
 
 def reaction_kernel(
@@ -169,16 +168,13 @@
             member = 2 * index + half
             source = lax.div(member, per_source)
             inner = lax.rem(member, per_source)
-            parts = []
-            for start in range(0, slots, WIDE):
-                fields = packed_ref[source, 0, inner, :, start : start + WIDE]
-                one = jnp.dot(in_ref[...], fields, preferred_element_type=jnp.float32)
-                one = half_silu(one + bias_one_ref[...])
-                two = jnp.dot(hid_ref[...], one, preferred_element_type=jnp.float32)
-                two = half_silu(two + bias_two_ref[...])
-                change = jnp.dot(coef_ref[member], two, preferred_element_type=jnp.float32)
-                parts.append(fields.astype(jnp.float32) + change * hidden ** (-0.5))
-            both.append(jnp.concatenate(parts, axis=1))
+            fields = packed_ref[source, 0, inner]
+            one = jnp.dot(in_ref[...], fields, preferred_element_type=jnp.float32)
+            one = half_silu(one + bias_one_ref[...])
+            two = jnp.dot(hid_ref[...], one, preferred_element_type=jnp.float32)
+            two = half_silu(two + bias_two_ref[...])
+            change = jnp.dot(coef_ref[member], two, preferred_element_type=jnp.float32)
+            both.append(fields.astype(jnp.float32) + change * hidden ** (-0.5))
         pair = jnp.concatenate(both, axis=0).astype(jnp.bfloat16)
         fresh[pl.ds(pl.multiple_of(index * 2 * tracers, 16), 2 * tracers)] = pair
         return carry

time: 242 us -> 200 us (0.83)
  Pallas kernels: 148 us -> 105 us
    pallas_call x2, Pallas kernels: 99.5 us -> 56.8 us  [reaction(): pl.pallas_call(functools.partial(reaction_kernel, first), grid=(part,), i...]
  transfers between devices with their start and end apart: 3 -> 3, of which waited for: 1 -> 1; matrix products, arithmetic and copies ran while one was open for 10% -> 12% of each run, Pallas kernels for 53% -> 43%
where the time goes in v3:
time: 200 us; the launch traced here: 199 us
  Pallas kernels  105 us (52%)
  local copies, waits for them, and re-layouts  23 us (12%)
  waiting for transfers between devices  17.3 us (9%)
  other arithmetic  16.4 us (8%)
  between operations  15 us (8%)
  starting transfers between devices  11.2 us (6%)
  blocking collectives  5.56 us (3%)
  matrix products  4.73 us (2%)
    pallas_call x2, Pallas kernels, reaction(): pl.pallas_call(functools.partial(reaction_kernel, first), grid=(part,), i...  56.8 us
    pallas_call x2, Pallas kernels, transport_packed(): pl.pallas_call(transport_kernel, grid=(lats,), in_specs=[pl.BlockSpec((fi...  38.8 us
    unnamed x60, local copies, waits for them, and re-layouts  18.6 us
    all_to_all x2, waiting for transfers between devices, shards(): lax.all_to_all(packed, 'trc', split_axis=0, concat_axis=0, tiled=True)  17.3 us
    all_to_all x2, starting transfers between devices, shards(): lax.all_to_all(packed, 'trc', split_axis=0, concat_axis=0, tiled=True)  11 us
    pallas_call x1, Pallas kernels, sum_over_blocks(): pl.pallas_call(functools.partial(sum_kernel, count), in_specs=[pl.BlockSp...  9.85 us
    another operation x3, other arithmetic, solve_system(): factor = jnp.linalg.cholesky(system)  6.55 us
    all_gather x1, blocking collectives, shards(): predicted_all = lax.all_gather(predicted_own, 'ens', axis=0, tiled=True)  5.56 us
  transfers between devices with their start and end apart: 3, of which 1 were waited for; matrix products, arithmetic and copies ran while one was open for 12% of the time, Pallas kernels for 43%

profile of v3, /device:TPU:0, one launch (start us, length us, event | category | flops | bytes accessed | tf_op | source)
XLA Modules:
  0.0 198.7 jit_solution(12958971338250302980)
XLA Ops:
  7.2 1.4 fusion.3
  8.7 19.8 %transport.3 = bf16[8,2,2,24,1152]{4,3,2,1,0:T(8,128)(2,1)} custom-call(bf16[48,4,8,1440]{3,2,1,0:T(8,128)(2,1)} %state_ref.3, f32[2,4,8,1440]{3,2,1,0:T(8,128)S(1)} %copy-done.17, s32[8,1440]{1,0:T(8,128)S(1)} %copy-done.18, s32[8,1,1536]{2,1,0:T(1,128)S(1)} %broadcast_in_dim.24.rank_ref), custom_call_target="tpu_custom_call" | custom-call | flops 2717908992 | bytes 4423680 | tf_op jit(solution)/shard_map/transport/pallas_call | solution.py:105
  28.4 7.4 %all-to-all-start.1 = ((bf16[8,2,2,24,1152]{4,3,2,1,0:T(8,128)(2,1)}), bf16[8,2,2,24,1152]{4,3,2,1,0:T(8,128)(2,1)S(1)}, u32[]{:S(2)}, u32[]{:S(2)}) async-start(bf16[8,2,2,24,1152]{4,3,2,1,0:T(8,128)(2,1)} %transport.3), calls=%async_computation.1 | async-start | bytes 3538944 | tf_op jit(solution)/shard_map/all_to_all | solution.py:350
  39.5 19.0 %transport.2 = bf16[8,2,2,24,1152]{4,3,2,1,0:T(8,128)(2,1)S(1)} custom-call(bf16[48,4,8,1440]{3,2,1,0:T(8,128)(2,1)} %state_ref.3, f32[2,4,8,1440]{3,2,1,0:T(8,128)S(1)} %copy-done.17, s32[8,1440]{1,0:T(8,128)S(1)} %copy-done.18, s32[8,1,1536]{2,1,0:T(1,128)S(1)} %copy.56.rank_ref), custom_call_target="tpu_custom_call" | custom-call | flops 2717908992 | bytes 4423680 | tf_op jit(solution)/shard_map/transport/pallas_call | solution.py:105
  58.5 1.2 copy-done
  59.8 17.3 %all-to-all-done.1.packed_ref = bf16[8,2,2,24,1152]{4,3,2,1,0:T(8,128)(2,1)S(1)} async-done(((bf16[8,2,2,24,1152]{4,3,2,1,0:T(8,128)(2,1)}), bf16[8,2,2,24,1152]{4,3,2,1,0:T(8,128)(2,1)S(1)}, u32[]{:S(2)}, u32[]{:S(2)}) %all-to-all-start.1) | async-done | bytes 1769504 | tf_op jit(solution)/shard_map/all_to_all | solution.py:350
  77.1 3.6 %all-to-all-start = ((bf16[8,2,2,24,1152]{4,3,2,1,0:T(8,128)(2,1)}), bf16[8,2,2,24,1152]{4,3,2,1,0:T(8,128)(2,1)S(1)}, u32[]{:S(2)}, u32[]{:S(2)}) async-start(bf16[8,2,2,24,1152]{4,3,2,1,0:T(8,128)(2,1)} %copy-done), calls=%async_computation | async-start | bytes 3538944 | tf_op jit(solution)/shard_map/all_to_all | solution.py:350
  80.9 1.9 copy.73
  82.8 1.2 copy.63.rank_ref
  85.6 1.4 copy.64.cell_ref
  88.3 1.1 copy-done.1
  89.4 0.9 copy-done.3
  91.3 0.9 copy-done.9
  92.2 1.0 copy-done.11
  94.8 28.4 %reaction.2 = (bf16[4,1440,384]{2,1,0:T(8,128)(2,1)}, f32[128,384]{1,0:T(8,128)S(1)}) custom-call(bf16[8,2,2,24,1152]{4,3,2,1,0:T(8,128)(2,1)S(1)} %all-to-all-done.1.packed_ref, bf16[256,24]{1,0:T(8,128)(2,1)S(1)} %copy-done.13, f32[256,1]{1,0:T(8,128)S(1)} %copy-done.9, bf16[256,256]{1,0:T(8,128)(2,1)S(1)} %copy-done.7, f32[256,1]{1,0:T(8,128)S(1)} %copy-done.11, ...), custom_call_target="tpu_custom_call" | custom-call | flops 8284667904 | bytes 3981312 | tf_op jit(solution)/shard_map/reaction/pallas_call | solution.py:209
  123.9 1.1 copy-done.2
  125.1 0.9 copy-done.4
  130.4 28.4 %reaction.3 = (bf16[4,1440,384]{2,1,0:T(8,128)(2,1)}, f32[128,384]{1,0:T(8,128)S(1)}) custom-call(bf16[8,2,2,24,1152]{4,3,2,1,0:T(8,128)(2,1)S(1)} %all-to-all-done.packed_ref, bf16[256,24]{1,0:T(8,128)(2,1)S(1)} %copy-done.14, f32[256,1]{1,0:T(8,128)S(1)} %copy-done.10, bf16[256,256]{1,0:T(8,128)(2,1)S(1)} %copy-done.8, ...), custom_call_target="tpu_custom_call", output_to_operand_aliasing={{0}: (8, {})} | custom-call | flops 8284667904 | bytes 3981312 | tf_op jit(solution)/shard_map/reaction/pallas_call | solution.py:209
  159.0 5.6 %all_gather.6 = bf16[64,6,128]{2,0,1:T(8,128)(2,1)S(1)} all-gather(bf16[16,6,128]{2,0,1:T(8,128)(2,1)S(1)} %copy.66), channel_id=1, replica_groups=mesh['ens'=4,'trc'=8] {'ens'}, dimensions={0}, use_global_device_ids=true | all-gather | bytes 122880 | tf_op jit(solution)/shard_map/all_gather | solution.py:372
  164.6 1.0 bitcast_subtract_fusion.1
  166.1 9.9 %block_sum.1 = f32[64,128]{1,0:T(8,128)S(1)} custom-call(f32[64,128]{1,0:T(8,128)S(1)} %fusion.4.term_ref), custom_call_target="tpu_custom_call" | custom-call | tf_op jit(solution)/shard_map/block_sum/pallas_call | solution.py:280
  176.1 5.8 %cholesky.16 = f32[64,64]{1,0:T(8,128)S(1)} custom-call(f32[64,64]{1,0:T(8,128)S(1)} %fusion.16), custom_call_target="Cholesky" | custom-call | tf_op jit(solution)/shard_map/jit(cholesky)/cholesky | solution.py:298
  183.3 4.9 %custom-call.8 = f32[1,64,64]{1,2,0:T(8,128)S(1)} custom-call(f32[1,64,64]{2,1,0:T(8,128)S(1)} %fusion.11), custom_call_target="InvertDiagBlocksLowerTriangular" | custom-call | tf_op jit(solution)/shard_map/triangular_solve | solution.py:300
  188.7 2.3 %convolution_add_fusion = f32[16,6144]{1,0:T(8,128)S(1)} fusion(f32[16,6144]{1,0:T(8,128)S(1)} %bitcast.61, f32[64,6144]{1,0:T(8,128)} %all-gather.2.cloned.1.call-done, f32[64,64]{0,1:T(8,128)S(1)} %fusion.12, s32[]{:T(128)S(6)} %select_n.17), kind=kOutput, calls=%fused_computation.2 | convolution fusion | flops 75595776 | bytes 2367492 | tf_op jit(solution)/shard_map/dot_general | solution.py:393
  (86 shorter events, 17.4 us)
Async XLA Ops:
  7.2 1.5 copy-start.18
  7.2 1.5 copy-start.17
  28.4 7.4 %copy-start.24 = (f32[1,6,128]{2,0,1:T(1,128)S(1)}, f32[1,6,128]{2,0,1:T(1,128)}, u32[]{:S(2)}) copy-start(f32[1,6,128]{2,0,1:T(1,128)} %param.23) | copy-start | bytes 9220
  28.4 7.5 %copy-start.21 = (f32[64,1,6,128]{3,1,2,0:T(1,128)S(1)}, f32[64,1,6,128]{3,1,2,0:T(1,128)}, u32[]{:S(2)}) copy-start(f32[64,1,6,128]{3,1,2,0:T(1,128)} %param.25) | copy-start | bytes 589828
  28.4 8.7 %copy-start.22 = (bf16[256,256]{1,0:T(8,128)(2,1)S(1)}, bf16[256,256]{1,0:T(8,128)(2,1)}, u32[]{:S(2)}) copy-start(bf16[256,256]{1,0:T(8,128)(2,1)} %param.18) | copy-start | bytes 393220
  28.4 8.8 %copy-start.20 = (f32[16,24,256]{2,1,0:T(8,128)S(1)}, f32[16,24,256]{2,1,0:T(8,128)}, u32[]{:S(2)}) copy-start(f32[16,24,256]{2,1,0:T(8,128)} %param.20) | copy-start | bytes 1179652
  28.4 48.6 %all-to-all-start.1 = ((bf16[8,2,2,24,1152]{4,3,2,1,0:T(8,128)(2,1)}), bf16[8,2,2,24,1152]{4,3,2,1,0:T(8,128)(2,1)S(1)}, u32[]{:S(2)}, u32[]{:S(2)}) async-start(bf16[8,2,2,24,1152]{4,3,2,1,0:T(8,128)(2,1)} %transport.3), calls=%async_computation.1 | async-start | bytes 3538944 | tf_op jit(solution)/shard_map/all_to_all | solution.py:350
  35.8 2.1 %copy-start.23 = (bf16[24,256]{1,0:T(8,128)(2,1)S(1)}, bf16[24,256]{1,0:T(8,128)(2,1)}, u32[]{:S(2)}) copy-start(bf16[24,256]{1,0:T(8,128)(2,1)} %param.16) | copy-start | bytes 36868
  35.8 2.3 %copy-start.25 = (f32[256]{0:T(256)S(1)}, f32[256]{0:T(256)}, u32[]{:S(2)}) copy-start(f32[256]{0:T(256)} %param.17) | copy-start | bytes 3076
  35.9 2.3 %copy-start.26 = (f32[256]{0:T(256)S(1)}, f32[256]{0:T(256)}, u32[]{:S(2)}) copy-start(f32[256]{0:T(256)} %param.19) | copy-start | bytes 3076
  58.5 1.2 copy-start
  77.1 46.9 %all-to-all-start = ((bf16[8,2,2,24,1152]{4,3,2,1,0:T(8,128)(2,1)}), bf16[8,2,2,24,1152]{4,3,2,1,0:T(8,128)(2,1)S(1)}, u32[]{:S(2)}, u32[]{:S(2)}) async-start(bf16[8,2,2,24,1152]{4,3,2,1,0:T(8,128)(2,1)} %copy-done), calls=%async_computation | async-start | bytes 3538944 | tf_op jit(solution)/shard_map/all_to_all | solution.py:350
  80.7 108.0 %all-gather.2.cloned.1.call-start = ((), (), s32[]{:S(2)}) async-start(), calls=%async_computation.2 | async-start | bytes 1966080 | tf_op jit(solution)/shard_map/all_gather | solution.py:339
  88.3 1.1 copy-start.1
  89.4 0.9 copy-start.3
  90.4 0.9 copy-start.7
  91.3 0.9 copy-start.9
  92.2 1.0 copy-start.11
  123.9 1.1 copy-start.2
  125.1 0.9 copy-start.4
  126.0 0.9 copy-start.8
  126.9 0.9 copy-start.10
  130.4 28.4 %copy-start.6 = (f32[128,384]{1,0:T(8,128)S(1)}, f32[128,384]{1,0:T(8,128)}, u32[]{:S(2)}) copy-start(f32[128,384]{1,0:T(8,128)} %copy-done.5) | copy-start | bytes 589828
  158.8 29.9 %copy-start.19 = (f32[2,8,24,256]{3,1,2,0:T(8,128)S(1)}, f32[2,8,24,256]{3,1,2,0:T(8,128)}, u32[]{:S(2)}) copy-start(f32[2,8,24,256]{3,1,2,0:T(8,128)} %copy.73) | copy-start | bytes 1179652
  (6 other events, 4.9 us)
Sparse Core Ops, SparseCore 0:
  83.7 21.0 all-gather.1
